TPU v7x, 32 devices: a whole 2x2x4 slice. The times are simulated.
32 devices in a mesh: grp: 2 (over x), ep: 8 (over z, y), sub: 2 (over core).
Axes of the slice: x: 2, y: 2, z: 4, core: 2. Of those that a mesh axis runs over, the one named last changes fastest.
Arguments:
- queries: bfloat16 [320, 16, 128], P(('grp', 'ep'), 'sub'), parts along dimension 0
- cache_keys: bfloat16 [320, 2, 384, 128], P(('grp', 'ep'), 'sub'), parts along dimension 0, may hold values from -6 to 6
- cache_values: bfloat16 [320, 2, 384, 128], P(('grp', 'ep'), 'sub'), parts along dimension 0, may hold values from -6 to 6
- new_keys: bfloat16 [320, 2, 128], P(('grp', 'ep'), 'sub'), parts along dimension 0
- new_values: bfloat16 [320, 2, 128], P(('grp', 'ep'), 'sub'), parts along dimension 0, may hold values from -6 to 6
- lengths: int32 [320], P(('grp', 'ep')), parts along dimension 0, may hold values from 1 to 384, as said below
- out_proj: bfloat16 [2048, 2048], P('sub'), may hold values from -1.5 to 1.5
- residual: bfloat16 [320, 2048], P(('grp', 'ep', 'sub')), parts along dimension 0, may hold values from -6 to 6
- norm_gain: float32 [2048], replicated, may hold values from 0.25 to 1.75
- gate_proj: bfloat16 [64, 2048, 768], P(('ep', 'sub')), may hold values from -0.125 to 0.125
- up_proj: bfloat16 [64, 2048, 768], P(('ep', 'sub')), may hold values from -0.125 to 0.125
- down_proj: bfloat16 [64, 768, 2048], P(('ep', 'sub')), may hold values from -0.21875 to 0.21875
- routing: int32 [320, 8], P(('grp', 'ep', 'sub')), parts along dimension 0, may hold values from 0 to 63, all different within a row; in each aligned block of 10 rows (0 to 9, 10 to 19, ...) at most 3 rows name the same one
- route_weights: float32 [320, 8], P(('grp', 'ep', 'sub')), parts along dimension 0, may hold values from 0.05 to 1
Outputs:
- layer_out: bfloat16 [320, 2048], P(('grp', 'ep', 'sub')), parts along dimension 0
There are 2 independent parts, one for each index of `grp`. A program takes and returns all parts, laid end to end along the dimension named above; an argument that names none is the same for every part. Nothing has to cross between parts.
Inputs may be any that keep to these rules, and one draw needn't show every extreme that they name: Slots 0 to lengths - 1 of a request are live; some request has exactly 384. `routing`: each request names 8 different experts; among the 10 requests of one device no expert is named by more than 3, and some device reaches 3.
All inputs are finite; a program needn't handle non-finite values.
Results may differ from a plain program's by a relative error of at most 0.007.
Values may be sent and summed in bfloat16 or wider, within the bound.
A program may use at most 128 MiB of HBM per device.

v0:
```python
import functools
import math

import jax
import jax.numpy as jnp
from jax import lax
from jax.experimental import pallas as pl
from jax.experimental.pallas import tpu as pltpu
from jax.sharding import PartitionSpec as P

PAD = 16
CHUNKS = 4
TILE = 256
MESH = pl.DeviceIdType.MESH
F32 = jnp.float32
BF16 = jnp.bfloat16


def kernel(
    n_ep, unroll,
    q_ref, nk_ref, nv_ref, len_ref, res_ref, gain_ref, route_ref, rw_ref,
    k_hbm, v_hbm, op_hbm, g_hbm, u_hbm, d_hbm,
    out_ref,
    k_s, v_s, op_s, g_s, u_s, d_s,
    ho, pr, prr, stream, w_own, w_all, xa, hid, part, r1, s1, r2, s2, r3,
    load_sem, g_sem, u_sem, d_sem, pr_sem, ws_sem, wr_sem,
    zs_sem, zr_sem, ys_sem, yr_sem, cs_sem, cr_sem,
    a_send, a_recv, b_send, b_recv, c_send, c_recv,
):
    nz = n_ep // 2
    n = n_ep * 2
    ep, sub = lax.axis_index("ep"), lax.axis_index("sub")
    hi, lo = ep // 2, ep % 2
    me = ep * 2 + sub
    rows, heads, hd = q_ref.shape
    half = rows // 2
    experts, width, ff = g_hbm.shape
    window = k_s.shape[1]

    def at(z, y, c):
        return {"ep": z * 2 + y, "sub": c}

    def remote(src, dst, ss, rs, where):
        return pltpu.make_async_remote_copy(
            src_ref=src, dst_ref=dst, send_sem=ss, recv_sem=rs,
            device_id=where, device_id_type=MESH,
        )

    k_cp = pltpu.make_async_copy(k_hbm, k_s, load_sem.at[0])
    v_cp = pltpu.make_async_copy(v_hbm, v_s, load_sem.at[1])
    op_cp = pltpu.make_async_copy(op_hbm, op_s, load_sem.at[2])
    k_cp.start()
    v_cp.start()
    op_cp.start()

    barrier = pltpu.get_barrier_semaphore()
    for k in range(1, n):
        peer = (me + k) % n
        pl.semaphore_signal(barrier, inc=1, device_id={"ep": peer // 2, "sub": peer % 2}, device_id_type=MESH)
    pl.semaphore_wait(barrier, n - 1)

    lanes = lax.broadcasted_iota(jnp.int32, (half, 128), 1)
    dense = jnp.zeros((half, 128), F32)
    for t in range(route_ref.shape[1]):
        dense = dense + jnp.where(route_ref[:, t : t + 1] == lanes, rw_ref[:, t : t + 1], 0.0)
    w_own[...] = jnp.zeros_like(w_own)
    w_own[0:half, :] = dense
    w_all[sub, lo, hi] = w_own[...]
    w_copies = []
    for k in range(1, n):
        peer = (me + k) % n
        cp = remote(w_own, w_all.at[sub, lo, hi], ws_sem.at[k], wr_sem.at[k], {"ep": peer // 2, "sub": peer % 2})
        cp.start()
        w_copies.append(cp)

    ho[...] = jnp.zeros_like(ho)
    k_cp.wait()
    v_cp.wait()
    for e in range(experts):
        pltpu.make_async_copy(g_hbm.at[e], g_s.at[e], g_sem.at[e]).start()
        pltpu.make_async_copy(u_hbm.at[e], u_s.at[e], u_sem.at[e]).start()
    for e in range(experts):
        pltpu.make_async_copy(d_hbm.at[e], d_s.at[e], d_sem.at[e]).start()

    scale = 1.0 / math.sqrt(hd)
    slots = lax.broadcasted_iota(jnp.int32, (heads, window), 1)

    def attend(i, carry):
        bs = [i * unroll + j for j in range(unroll)]
        qs = [q_ref[b] for b in bs]
        ss = [
            lax.dot_general(q, k_s[b], (((1,), (1,)), ((), ())), preferred_element_type=F32) * scale
            for q, b in zip(qs, bs)
        ]
        owns = [
            jnp.sum(q.astype(F32) * nk_ref[b].astype(F32), -1, keepdims=True) * scale for q, b in zip(qs, bs)
        ]
        ss = [jnp.where(slots < len_ref[b], s, -1e30) for s, b in zip(ss, bs)]
        tops = [jnp.maximum(jnp.max(s, -1, keepdims=True), o) for s, o in zip(ss, owns)]
        ws = [jnp.exp(s - t) for s, t in zip(ss, tops)]
        os = [jnp.exp(o - t) for o, t in zip(owns, tops)]
        dens = [jnp.sum(w, -1, keepdims=True) + o for w, o in zip(ws, os)]
        mixes = [
            jnp.dot(w.astype(BF16), v_s[b], preferred_element_type=F32)
            + o.astype(BF16).astype(F32) * nv_ref[b].astype(F32)
            for w, o, b in zip(ws, os, bs)
        ]
        for m, d, b in zip(mixes, dens, bs):
            ho[(b // half) * PAD + b % half] = m / d
        return carry

    lax.fori_loop(0, rows // unroll, attend, 0)

    flat = jnp.concatenate([ho[:, h, :] for h in range(heads)], axis=1).astype(BF16)
    op_cp.wait()
    piece = width // CHUNKS

    def project(j, carry):
        cols = pl.ds(pl.multiple_of(j * piece, piece), piece)
        p = jnp.dot(flat, op_s[:, cols], preferred_element_type=F32)
        pr[0, :, cols] = p[:PAD]
        pr[1, :, cols] = p[PAD:]
        return carry

    lax.fori_loop(0, CHUNKS, project, 0)
    pr_cp = remote(pr.at[1 - sub], prr, pr_sem.at[0], pr_sem.at[1], at(hi, lo, 1 - sub))
    pr_cp.start()
    pr_cp.wait()
    stream[...] = pr[sub] + prr[...]
    stream[0:half, :] = stream[0:half, :] + res_ref[...].astype(F32)
    x = stream[...]
    normed = x * lax.rsqrt(jnp.mean(x * x, -1, keepdims=True) + 1e-6) * gain_ref[...]
    xa[sub, lo, hi] = normed.astype(BF16)

    sends = []

    def go(src, ss, rs, where):
        cp = remote(src, src, ss, rs, where)
        cp.start()
        sends.append(cp)

    for k in range(1, nz):
        go(xa.at[sub, lo, hi], zs_sem.at[k], zr_sem.at[k], at((hi + k) % nz, lo, sub))
    go(xa.at[sub, lo, hi], ys_sem.at[0], yr_sem.at[0], at(hi, 1 - lo, sub))
    go(xa.at[sub, lo, hi], cs_sem.at[0, 0], cr_sem.at[0, 0], at(hi, lo, 1 - sub))

    def landed(c, y, k, rs):
        ref = xa.at[c, y, (hi - k + nz) % nz]
        remote(ref, ref, rs, rs, at(hi, lo, 1 - sub)).wait_recv()
        return ref

    for k in range(1, nz):
        ref = landed(sub, lo, k, zr_sem.at[k])
        go(ref, ys_sem.at[k], yr_sem.at[k], at(hi, 1 - lo, sub))
        go(ref, cs_sem.at[0, k], cr_sem.at[0, k], at(hi, lo, 1 - sub))
    for k in range(nz):
        ref = landed(sub, 1 - lo, k, yr_sem.at[k])
        go(ref, cs_sem.at[1, k], cr_sem.at[1, k], at(hi, lo, 1 - sub))
    for k in range(nz):
        landed(1 - sub, lo, k, cr_sem.at[0, k])
        landed(1 - sub, 1 - lo, k, cr_sem.at[1, k])
    for cp in w_copies:
        cp.wait()

    total = n * PAD
    tiles = ff // TILE
    lane = lax.broadcasted_iota(jnp.int32, (total, 128), 1)

    def expert(e, carry):
        pltpu.make_async_copy(g_hbm.at[e], g_s.at[e], g_sem.at[e]).wait()
        pltpu.make_async_copy(u_hbm.at[e], u_s.at[e], u_sem.at[e]).wait()
        w_e = jnp.sum(jnp.where(lane == me * experts + e, w_all[...].reshape(total, 128), 0.0), -1, keepdims=True)

        def tile(t, carry):
            cols = pl.ds(pl.multiple_of(t * TILE, TILE), TILE)
            xs = xa[...].reshape(total, width)
            g = jnp.dot(xs, g_s[e, :, cols], preferred_element_type=F32)
            u = jnp.dot(xs, u_s[e, :, cols], preferred_element_type=F32)
            h = (g / (1.0 + jnp.exp(-g))) * u * w_e
            hid[:, pl.ds(pl.multiple_of(e * ff + t * TILE, TILE), TILE)] = h.astype(BF16)
            return carry

        return lax.fori_loop(0, tiles, tile, carry)

    lax.fori_loop(0, experts, expert, 0)
    for e in range(experts):
        pltpu.make_async_copy(d_hbm.at[e], d_s.at[e], d_sem.at[e]).wait()

    firsts, seconds, thirds = {}, {}, {}

    def down(j):
        acc = jnp.dot(
            hid[...],
            d_s[:, :, j * piece : (j + 1) * piece].reshape(experts * ff, piece),
            preferred_element_type=F32,
        )
        part[j] = acc.astype(BF16).reshape(2, 2, nz, PAD, piece)
        firsts[j] = remote(part.at[j, 1 - sub], r1.at[j], a_send.at[j], a_recv.at[j], at(hi, lo, 1 - sub))
        firsts[j].start()

    def second(j):
        firsts[j].wait()
        s1[j] = (part[j, sub].astype(F32) + r1[j].astype(F32)).astype(BF16)
        seconds[j] = remote(s1.at[j, 1 - lo], r2.at[j], b_send.at[j], b_recv.at[j], at(hi, 1 - lo, sub))
        seconds[j].start()

    def third(j):
        seconds[j].wait()
        s2[j] = (s1[j, lo].astype(F32) + r2[j].astype(F32)).astype(BF16)
        thirds[j] = []
        for k in range(1, nz):
            z = (hi + k) % nz
            cp = remote(s2.at[j, z], r3.at[j, k], c_send.at[j, k], c_recv.at[j, k], at(z, lo, sub))
            cp.start()
            thirds[j].append(cp)

    def final(j):
        acc = s2[j, hi].astype(F32)
        for k in range(1, nz):
            thirds[j][k - 1].wait()
            acc = acc + r3[j, k].astype(F32)
        acc = acc + stream[:, j * piece : (j + 1) * piece]
        out_ref[:, j * piece : (j + 1) * piece] = acc[:half].astype(out_ref.dtype)

    for step in range(CHUNKS + 3):
        if step < CHUNKS:
            down(step)
        for lag, stage in ((1, second), (2, third), (3, final)):
            if 0 <= step - lag < CHUNKS:
                stage(step - lag)
    for cp in sends:
        cp.wait_send()


def per_device(
    queries, cache_keys, cache_values, new_keys, new_values, lengths, out_proj, residual,
    norm_gain, gate_proj, up_proj, down_proj, routing, route_weights,
):
    n_ep = lax.axis_size("ep")
    rows, heads, hd = queries.shape
    window = cache_keys.shape[2]
    half, width = residual.shape
    experts, _, ff = gate_proj.shape
    nz, n = n_ep // 2, n_ep * 2
    piece = width // CHUNKS
    unroll = next(u for u in (5, 4, 2, 1) if rows % u == 0)
    vmem = pl.BlockSpec(memory_space=pltpu.VMEM)
    hbm = pl.BlockSpec(memory_space=pl.ANY)
    dma = pltpu.SemaphoreType.DMA
    return pl.pallas_call(
        functools.partial(kernel, n_ep, unroll),
        out_shape=jax.ShapeDtypeStruct((half, width), BF16),
        in_specs=[vmem] * 3 + [pl.BlockSpec(memory_space=pltpu.SMEM)] + [vmem] * 4 + [hbm] * 6,
        out_specs=vmem,
        scratch_shapes=[
            pltpu.VMEM((rows, window, hd), BF16),
            pltpu.VMEM((rows, window, hd), BF16),
            pltpu.VMEM(out_proj.shape, BF16),
            pltpu.VMEM(gate_proj.shape, BF16),
            pltpu.VMEM(up_proj.shape, BF16),
            pltpu.VMEM(down_proj.shape, BF16),
            pltpu.VMEM((2 * PAD, heads, hd), F32),
            pltpu.VMEM((2, PAD, width), F32),
            pltpu.VMEM((PAD, width), F32),
            pltpu.VMEM((PAD, width), F32),
            pltpu.VMEM((PAD, 128), F32),
            pltpu.VMEM((2, 2, nz, PAD, 128), F32),
            pltpu.VMEM((2, 2, nz, PAD, width), BF16),
            pltpu.VMEM((n * PAD, experts * ff), BF16),
            pltpu.VMEM((CHUNKS, 2, 2, nz, PAD, piece), BF16),
            pltpu.VMEM((CHUNKS, 2, nz, PAD, piece), BF16),
            pltpu.VMEM((CHUNKS, 2, nz, PAD, piece), BF16),
            pltpu.VMEM((CHUNKS, nz, PAD, piece), BF16),
            pltpu.VMEM((CHUNKS, nz, PAD, piece), BF16),
            pltpu.VMEM((CHUNKS, nz, PAD, piece), BF16),
            dma((3,)), dma((experts,)), dma((experts,)), dma((experts,)), dma((2,)), dma((n,)), dma((n,)),
            dma((nz,)), dma((nz,)), dma((nz,)), dma((nz,)), dma((2, nz)), dma((2, nz)),
            dma((CHUNKS,)), dma((CHUNKS,)), dma((CHUNKS,)), dma((CHUNKS,)), dma((CHUNKS, nz)), dma((CHUNKS, nz)),
        ],
        compiler_params=pltpu.CompilerParams(
            collective_id=0, has_side_effects=True, vmem_limit_bytes=60 * 1024 * 1024
        ),
    )(
        queries, new_keys, new_values, lengths, residual, norm_gain.reshape(1, width), routing, route_weights,
        cache_keys.reshape(rows, window, hd), cache_values.reshape(rows, window, hd), out_proj,
        gate_proj, up_proj, down_proj,
    )


def solution(mesh):
    return jax.shard_map(
        per_device,
        mesh=mesh,
        in_specs=(
            P(("grp", "ep"), "sub", None),
            P(("grp", "ep"), "sub", None, None),
            P(("grp", "ep"), "sub", None, None),
            P(("grp", "ep"), "sub", None),
            P(("grp", "ep"), "sub", None),
            P(("grp", "ep")),
            P("sub", None),
            P(("grp", "ep", "sub"), None),
            P(),
            P(("ep", "sub"), None, None),
            P(("ep", "sub"), None, None),
            P(("ep", "sub"), None, None),
            P(("grp", "ep", "sub"), None),
            P(("grp", "ep", "sub"), None),
        ),
        out_specs=P(("grp", "ep", "sub"), None),
        check_vma=False,
    )
```

profile of v0, /device:TPU:0, one launch (start us, length us, event | category | flops | bytes accessed | tf_op | source)
XLA Modules:
  0.0 58.4 jit_solution(4346974905278419982)
XLA Ops:
  0.0 1.4 %copy.17.route_ref = s32[10,8]{1,0:T(8,128)} copy(s32[10,8]{0,1:T(8,128)} %param.26) | data formatting | bytes 640 | tf_op args[12]
  1.4 1.4 %copy.18.rw_ref = f32[10,8]{1,0:T(8,128)} copy(f32[10,8]{0,1:T(8,128)} %param.27) | data formatting | bytes 640 | tf_op args[13]
  2.7 1.3 %copy.15.nk_ref = bf16[20,1,128]{2,1,0:T(2,128)(2,1)} copy(bf16[20,1,128]{2,0,1:T(8,128)(2,1)} %param.17) | data formatting | bytes 10240 | tf_op args[3]
  4.0 1.3 %copy.16.nv_ref = bf16[20,1,128]{2,1,0:T(2,128)(2,1)} copy(bf16[20,1,128]{2,0,1:T(8,128)(2,1)} %param.18) | data formatting | bytes 10240 | tf_op args[4]
  5.3 51.7 %shard_map.136 = bf16[10,2048]{1,0:T(8,128)(2,1)} custom-call(bf16[20,8,128]{2,1,0:T(8,128)(2,1)} %q_ref.1, bf16[20,1,128]{2,1,0:T(2,128)(2,1)} %copy.15.nk_ref, bf16[20,1,128]{2,1,0:T(2,128)(2,1)} %copy.16.nv_ref, s32[20]{0:T(128)} %len_ref.1, bf16[10,2048]{1,0:T(8,128)(2,1)} %res_ref.1, f32[1,2048]{1,0:T(1,128)} %bitcast.5, s32[10,8]{1,0:T(8,128)} %copy.17.route_ref, ...), custom_call_target="tpu_custom_call" | custom-call | tf_op jit(solution)/shard_map/pallas_call | solution.py:250
  57.0 1.5 %copy.20 = bf16[10,2048]{1,0:T(8,128)(2,1)} copy(bf16[10,2048]{1,0:T(8,128)(2,1)} %shard_map.136) | data formatting | bytes 81920
where the time goes:
time: 58.8 us; the launch traced here: 58.4 us
  Pallas kernels  51.7 us (88%)
  local copies, waits for them, and re-layouts  6.78 us (12%)
    pallas_call x1, Pallas kernels, per_device(): pl.pallas_call(functools.partial(kernel, n_ep, unroll), out_shape=jax.Sha...  51.7 us
    unnamed x5, local copies, waits for them, and re-layouts  6.78 us

commit v1 on v0

--- a/solution.py
+++ b/solution.py
@@ -9,7 +9,8 @@
 from jax.sharding import PartitionSpec as P
 
 PAD = 16
-CHUNKS = 4
+CHUNKS = 2
+PARTS = 2
 TILE = 256
 MESH = pl.DeviceIdType.MESH
 F32 = jnp.float32
@@ -22,7 +23,7 @@
     k_hbm, v_hbm, op_hbm, g_hbm, u_hbm, d_hbm,
     out_ref,
     k_s, v_s, op_s, g_s, u_s, d_s,
-    ho, pr, prr, stream, w_own, w_all, xa, hid, part, r1, s1, r2, s2, r3,
+    ho, pr, prr, stream, w_own, w_all, w_row, nk, nv, xa, xc, hid, part, r1, s1, r2, s2, r3,
     load_sem, g_sem, u_sem, d_sem, pr_sem, ws_sem, wr_sem,
     zs_sem, zr_sem, ys_sem, yr_sem, cs_sem, cr_sem,
     a_send, a_recv, b_send, b_recv, c_send, c_recv,
@@ -59,12 +60,13 @@
         pl.semaphore_signal(barrier, inc=1, device_id={"ep": peer // 2, "sub": peer % 2}, device_id_type=MESH)
     pl.semaphore_wait(barrier, n - 1)
 
-    lanes = lax.broadcasted_iota(jnp.int32, (half, 128), 1)
-    dense = jnp.zeros((half, 128), F32)
-    for t in range(route_ref.shape[1]):
-        dense = dense + jnp.where(route_ref[:, t : t + 1] == lanes, rw_ref[:, t : t + 1], 0.0)
-    w_own[...] = jnp.zeros_like(w_own)
-    w_own[0:half, :] = dense
+    ids = lax.broadcasted_iota(jnp.int32, (128, half), 0)
+    dense = jnp.zeros((128, half), F32)
+    for t in range(route_ref.shape[0]):
+        dense = dense + jnp.where(route_ref[t : t + 1, :] == ids, rw_ref[t : t + 1, :], 0.0)
+    w_row[...] = jnp.zeros_like(w_row)
+    w_row[0:128, 0:half] = dense
+    w_own[...] = w_row[0:128, 0:128].T[0:PAD]
     w_all[sub, lo, hi] = w_own[...]
     w_copies = []
     for k in range(1, n):
@@ -81,6 +83,8 @@
         pltpu.make_async_copy(u_hbm.at[e], u_s.at[e], u_sem.at[e]).start()
     for e in range(experts):
         pltpu.make_async_copy(d_hbm.at[e], d_s.at[e], d_sem.at[e]).start()
+    nk[...] = nk_ref[...].astype(F32)
+    nv[...] = nv_ref[...].astype(F32)
 
     scale = 1.0 / math.sqrt(hd)
     slots = lax.broadcasted_iota(jnp.int32, (heads, window), 1)
@@ -93,7 +97,7 @@
             for q, b in zip(qs, bs)
         ]
         owns = [
-            jnp.sum(q.astype(F32) * nk_ref[b].astype(F32), -1, keepdims=True) * scale for q, b in zip(qs, bs)
+            jnp.sum(q.astype(F32) * nk[pl.ds(b, 1), :], -1, keepdims=True) * scale for q, b in zip(qs, bs)
         ]
         ss = [jnp.where(slots < len_ref[b], s, -1e30) for s, b in zip(ss, bs)]
         tops = [jnp.maximum(jnp.max(s, -1, keepdims=True), o) for s, o in zip(ss, owns)]
@@ -102,7 +106,7 @@
         dens = [jnp.sum(w, -1, keepdims=True) + o for w, o in zip(ws, os)]
         mixes = [
             jnp.dot(w.astype(BF16), v_s[b], preferred_element_type=F32)
-            + o.astype(BF16).astype(F32) * nv_ref[b].astype(F32)
+            + o.astype(BF16).astype(F32) * nv[pl.ds(b, 1), :]
             for w, o, b in zip(ws, os, bs)
         ]
         for m, d, b in zip(mixes, dens, bs):
@@ -130,7 +134,9 @@
     stream[0:half, :] = stream[0:half, :] + res_ref[...].astype(F32)
     x = stream[...]
     normed = x * lax.rsqrt(jnp.mean(x * x, -1, keepdims=True) + 1e-6) * gain_ref[...]
-    xa[sub, lo, hi] = normed.astype(BF16)
+    cut = width // PARTS
+    for p in range(PARTS):
+        xa[p, sub, lo, hi] = normed[:, p * cut : (p + 1) * cut].astype(BF16)
 
     sends = []
 
@@ -139,41 +145,59 @@
         cp.start()
         sends.append(cp)
 
-    for k in range(1, nz):
-        go(xa.at[sub, lo, hi], zs_sem.at[k], zr_sem.at[k], at((hi + k) % nz, lo, sub))
-    go(xa.at[sub, lo, hi], ys_sem.at[0], yr_sem.at[0], at(hi, 1 - lo, sub))
-    go(xa.at[sub, lo, hi], cs_sem.at[0, 0], cr_sem.at[0, 0], at(hi, lo, 1 - sub))
-
-    def landed(c, y, k, rs):
-        ref = xa.at[c, y, (hi - k + nz) % nz]
+    for p in range(PARTS):
+        own = xa.at[p, sub, lo, hi]
+        for k in range(1, nz):
+            go(own, zs_sem.at[p, k], zr_sem.at[p, k], at((hi + k) % nz, lo, sub))
+        go(own, ys_sem.at[p, 0], yr_sem.at[p, 0], at(hi, 1 - lo, sub))
+        go(own, cs_sem.at[p, 0, 0], cr_sem.at[p, 0, 0], at(hi, lo, 1 - sub))
+
+    def landed(p, c, y, k, rs):
+        ref = xa.at[p, c, y, (hi - k + nz) % nz]
         remote(ref, ref, rs, rs, at(hi, lo, 1 - sub)).wait_recv()
         return ref
 
-    for k in range(1, nz):
-        ref = landed(sub, lo, k, zr_sem.at[k])
-        go(ref, ys_sem.at[k], yr_sem.at[k], at(hi, 1 - lo, sub))
-        go(ref, cs_sem.at[0, k], cr_sem.at[0, k], at(hi, lo, 1 - sub))
-    for k in range(nz):
-        ref = landed(sub, 1 - lo, k, yr_sem.at[k])
-        go(ref, cs_sem.at[1, k], cr_sem.at[1, k], at(hi, lo, 1 - sub))
-    for k in range(nz):
-        landed(1 - sub, lo, k, cr_sem.at[0, k])
-        landed(1 - sub, 1 - lo, k, cr_sem.at[1, k])
+    for p in range(PARTS):
+        for k in range(1, nz):
+            ref = landed(p, sub, lo, k, zr_sem.at[p, k])
+            go(ref, ys_sem.at[p, k], yr_sem.at[p, k], at(hi, 1 - lo, sub))
+            go(ref, cs_sem.at[p, 0, k], cr_sem.at[p, 0, k], at(hi, lo, 1 - sub))
+    for p in range(PARTS):
+        for k in range(nz):
+            ref = landed(p, sub, 1 - lo, k, yr_sem.at[p, k])
+            go(ref, cs_sem.at[p, 1, k], cr_sem.at[p, 1, k], at(hi, lo, 1 - sub))
+    for p in range(PARTS):
+        for k in range(nz):
+            landed(p, 1 - sub, lo, k, cr_sem.at[p, 0, k])
+            landed(p, 1 - sub, 1 - lo, k, cr_sem.at[p, 1, k])
     for cp in w_copies:
         cp.wait()
 
-    total = n * PAD
+    total = n * half
+    slots_all = n * PAD
+    r_id = lax.broadcasted_iota(jnp.int32, (total, slots_all), 0)
+    p_id = lax.broadcasted_iota(jnp.int32, (total, slots_all), 1)
+    pick = ((p_id // PAD) * half + p_id % PAD == r_id) & (p_id % PAD < half)
+    pick = jnp.where(pick, 1.0, 0.0).astype(BF16)
+    for p in range(PARTS):
+        packed = jnp.dot(pick, xa[p].reshape(slots_all, cut), preferred_element_type=F32)
+        xc[:, p * cut : (p + 1) * cut] = packed.astype(BF16)
+    for c in range(2):
+        for y in range(2):
+            for z in range(nz):
+                at_row = ((c * 2 + y) * nz + z) * half
+                w_row[at_row : at_row + half, :] = w_all[c, y, z, 0:half, :]
     tiles = ff // TILE
     lane = lax.broadcasted_iota(jnp.int32, (total, 128), 1)
 
     def expert(e, carry):
         pltpu.make_async_copy(g_hbm.at[e], g_s.at[e], g_sem.at[e]).wait()
         pltpu.make_async_copy(u_hbm.at[e], u_s.at[e], u_sem.at[e]).wait()
-        w_e = jnp.sum(jnp.where(lane == me * experts + e, w_all[...].reshape(total, 128), 0.0), -1, keepdims=True)
+        w_e = jnp.sum(jnp.where(lane == me * experts + e, w_row[0:total, :], 0.0), -1, keepdims=True)
 
         def tile(t, carry):
             cols = pl.ds(pl.multiple_of(t * TILE, TILE), TILE)
-            xs = xa[...].reshape(total, width)
+            xs = xc[...]
             g = jnp.dot(xs, g_s[e, :, cols], preferred_element_type=F32)
             u = jnp.dot(xs, u_s[e, :, cols], preferred_element_type=F32)
             h = (g / (1.0 + jnp.exp(-g))) * u * w_e
@@ -187,6 +211,17 @@
         pltpu.make_async_copy(d_hbm.at[e], d_s.at[e], d_sem.at[e]).wait()
 
     firsts, seconds, thirds = {}, {}, {}
+    quarter = nz * half
+    wide = s1.shape[2]
+
+    def spread(groups, step, wider):
+        shape = (groups * wider, groups * step)
+        o_id = lax.broadcasted_iota(jnp.int32, shape, 0)
+        i_id = lax.broadcasted_iota(jnp.int32, shape, 1)
+        hit = ((o_id // wider) * step + o_id % wider == i_id) & (o_id % wider < step)
+        return jnp.where(hit, 1.0, 0.0).astype(BF16)
+
+    by_y, by_z = spread(2, quarter, wide), spread(nz, half, PAD)
 
     def down(j):
         acc = jnp.dot(
@@ -194,19 +229,21 @@
             d_s[:, :, j * piece : (j + 1) * piece].reshape(experts * ff, piece),
             preferred_element_type=F32,
         )
-        part[j] = acc.astype(BF16).reshape(2, 2, nz, PAD, piece)
+        part[j] = acc.astype(BF16).reshape(2, 2 * quarter, piece)
         firsts[j] = remote(part.at[j, 1 - sub], r1.at[j], a_send.at[j], a_recv.at[j], at(hi, lo, 1 - sub))
         firsts[j].start()
 
     def second(j):
         firsts[j].wait()
-        s1[j] = (part[j, sub].astype(F32) + r1[j].astype(F32)).astype(BF16)
+        both = (part[j, sub].astype(F32) + r1[j].astype(F32)).astype(BF16)
+        s1[j] = jnp.dot(by_y, both, preferred_element_type=F32).astype(BF16).reshape(2, wide, piece)
         seconds[j] = remote(s1.at[j, 1 - lo], r2.at[j], b_send.at[j], b_recv.at[j], at(hi, 1 - lo, sub))
         seconds[j].start()
 
     def third(j):
         seconds[j].wait()
-        s2[j] = (s1[j, lo].astype(F32) + r2[j].astype(F32)).astype(BF16)
+        both = (s1[j, lo].astype(F32) + r2[j].astype(F32))[:quarter].astype(BF16)
+        s2[j] = jnp.dot(by_z, both, preferred_element_type=F32).astype(BF16).reshape(nz, PAD, piece)
         thirds[j] = []
         for k in range(1, nz):
             z = (hi + k) % nz
@@ -243,6 +280,7 @@
     experts, _, ff = gate_proj.shape
     nz, n = n_ep // 2, n_ep * 2
     piece = width // CHUNKS
+    wide = -(-nz * half // PAD) * PAD
     unroll = next(u for u in (5, 4, 2, 1) if rows % u == 0)
     vmem = pl.BlockSpec(memory_space=pltpu.VMEM)
     hbm = pl.BlockSpec(memory_space=pl.ANY)
@@ -265,23 +303,28 @@
             pltpu.VMEM((PAD, width), F32),
             pltpu.VMEM((PAD, 128), F32),
             pltpu.VMEM((2, 2, nz, PAD, 128), F32),
-            pltpu.VMEM((2, 2, nz, PAD, width), BF16),
-            pltpu.VMEM((n * PAD, experts * ff), BF16),
-            pltpu.VMEM((CHUNKS, 2, 2, nz, PAD, piece), BF16),
-            pltpu.VMEM((CHUNKS, 2, nz, PAD, piece), BF16),
-            pltpu.VMEM((CHUNKS, 2, nz, PAD, piece), BF16),
-            pltpu.VMEM((CHUNKS, nz, PAD, piece), BF16),
+            pltpu.VMEM((max(128, n * half), 128), F32),
+            pltpu.VMEM((rows, hd), F32),
+            pltpu.VMEM((rows, hd), F32),
+            pltpu.VMEM((PARTS, 2, 2, nz, PAD, width // PARTS), BF16),
+            pltpu.VMEM((n * half, width), BF16),
+            pltpu.VMEM((n * half, experts * ff), BF16),
+            pltpu.VMEM((CHUNKS, 2, n_ep * half, piece), BF16),
+            pltpu.VMEM((CHUNKS, n_ep * half, piece), BF16),
+            pltpu.VMEM((CHUNKS, 2, wide, piece), BF16),
+            pltpu.VMEM((CHUNKS, wide, piece), BF16),
             pltpu.VMEM((CHUNKS, nz, PAD, piece), BF16),
             pltpu.VMEM((CHUNKS, nz, PAD, piece), BF16),
             dma((3,)), dma((experts,)), dma((experts,)), dma((experts,)), dma((2,)), dma((n,)), dma((n,)),
-            dma((nz,)), dma((nz,)), dma((nz,)), dma((nz,)), dma((2, nz)), dma((2, nz)),
+            dma((PARTS, nz)), dma((PARTS, nz)), dma((PARTS, nz)), dma((PARTS, nz)), dma((PARTS, 2, nz)), dma((PARTS, 2, nz)),
             dma((CHUNKS,)), dma((CHUNKS,)), dma((CHUNKS,)), dma((CHUNKS,)), dma((CHUNKS, nz)), dma((CHUNKS, nz)),
         ],
         compiler_params=pltpu.CompilerParams(
             collective_id=0, has_side_effects=True, vmem_limit_bytes=60 * 1024 * 1024
         ),
     )(
-        queries, new_keys, new_values, lengths, residual, norm_gain.reshape(1, width), routing, route_weights,
+        queries, new_keys.transpose(1, 0, 2).reshape(rows, hd), new_values.transpose(1, 0, 2).reshape(rows, hd),
+        lengths, residual, norm_gain.reshape(1, width), routing.T, route_weights.T,
         cache_keys.reshape(rows, window, hd), cache_values.reshape(rows, window, hd), out_proj,
         gate_proj, up_proj, down_proj,
     )

time: 58.8 us -> 48.4 us (0.82)
  local copies, waits for them, and re-layouts: 6.78 us -> 1.47 us
  Pallas kernels: 51.7 us -> 46.7 us
    unnamed x5 -> x1, local copies, waits for them, and re-layouts: 6.78 us -> 1.47 us
    pallas_call x1, Pallas kernels: 51.7 us -> 46.7 us  [per_device(): pl.pallas_call(functools.partial(kernel, n_ep, unroll), out_shape=jax.Sha...]
where the time goes in v1:
time: 48.4 us; the launch traced here: 48.2 us
  Pallas kernels  46.7 us (96%)
  local copies, waits for them, and re-layouts  1.47 us (3%)
    pallas_call x1, Pallas kernels, per_device(): pl.pallas_call(functools.partial(kernel, n_ep, unroll), out_shape=jax.Sha...  46.7 us
    unnamed x1, local copies, waits for them, and re-layouts  1.47 us

profile of v1, /device:TPU:0, one launch (start us, length us, event | category | flops | bytes accessed | tf_op | source)
XLA Modules:
  0.0 48.2 jit_solution(16257955717864264673)
XLA Ops:
  0.0 46.7 %shard_map.136 = bf16[10,2048]{1,0:T(8,128)(2,1)} custom-call(bf16[20,8,128]{2,1,0:T(8,128)(2,1)} %q_ref.1, bf16[20,128]{1,0:T(8,128)(2,1)} %bitcast.10, bf16[20,128]{1,0:T(8,128)(2,1)} %bitcast.11, s32[20]{0:T(128)} %len_ref.1, bf16[10,2048]{1,0:T(8,128)(2,1)} %res_ref.1, f32[1,2048]{1,0:T(1,128)} %bitcast.9, s32[8,10]{1,0:T(8,128)} %bitcast.12, ...), custom_call_target="tpu_custom_call" | custom-call | tf_op jit(solution)/shard_map/pallas_call | solution.py:288
  46.7 1.5 %copy.16 = bf16[10,2048]{1,0:T(8,128)(2,1)} copy(bf16[10,2048]{1,0:T(8,128)(2,1)} %shard_map.136) | data formatting | bytes 81920

commit v2 on v1

--- a/solution.py
+++ b/solution.py
@@ -157,15 +157,18 @@
         remote(ref, ref, rs, rs, at(hi, lo, 1 - sub)).wait_recv()
         return ref
 
+    def across(p, k):
+        ref = landed(p, sub, 1 - lo, k, yr_sem.at[p, k])
+        go(ref, cs_sem.at[p, 1, k], cr_sem.at[p, 1, k], at(hi, lo, 1 - sub))
+
     for p in range(PARTS):
         for k in range(1, nz):
             ref = landed(p, sub, lo, k, zr_sem.at[p, k])
             go(ref, ys_sem.at[p, k], yr_sem.at[p, k], at(hi, 1 - lo, sub))
             go(ref, cs_sem.at[p, 0, k], cr_sem.at[p, 0, k], at(hi, lo, 1 - sub))
-    for p in range(PARTS):
-        for k in range(nz):
-            ref = landed(p, sub, 1 - lo, k, yr_sem.at[p, k])
-            go(ref, cs_sem.at[p, 1, k], cr_sem.at[p, 1, k], at(hi, lo, 1 - sub))
+            across(p, k - 1)
+    for p in range(PARTS):
+        across(p, nz - 1)
     for p in range(PARTS):
         for k in range(nz):
             landed(p, 1 - sub, lo, k, cr_sem.at[p, 0, k])

time: 48.4 us -> 51.3 us (1.060)
  Pallas kernels: 46.7 us -> 49.7 us
    pallas_call x1, Pallas kernels: 46.7 us -> 49.7 us  [per_device(): pl.pallas_call(functools.partial(kernel, n_ep, unroll), out_shape=jax.Sha...]
where the time goes in v2:
time: 51.3 us; the launch traced here: 51.1 us
  Pallas kernels  49.7 us (97%)
  local copies, waits for them, and re-layouts  1.47 us (3%)
    pallas_call x1, Pallas kernels, per_device(): pl.pallas_call(functools.partial(kernel, n_ep, unroll), out_shape=jax.Sha...  49.7 us
    unnamed x1, local copies, waits for them, and re-layouts  1.47 us

profile of v2, /device:TPU:0, one launch (start us, length us, event | category | flops | bytes accessed | tf_op | source)
XLA Modules:
  0.0 51.1 jit_solution(16601447001370047081)
XLA Ops:
  0.0 49.7 %shard_map.136 = bf16[10,2048]{1,0:T(8,128)(2,1)} custom-call(bf16[20,8,128]{2,1,0:T(8,128)(2,1)} %q_ref.1, bf16[20,128]{1,0:T(8,128)(2,1)} %bitcast.10, bf16[20,128]{1,0:T(8,128)(2,1)} %bitcast.11, s32[20]{0:T(128)} %len_ref.1, bf16[10,2048]{1,0:T(8,128)(2,1)} %res_ref.1, f32[1,2048]{1,0:T(1,128)} %bitcast.9, s32[8,10]{1,0:T(8,128)} %bitcast.12, ...), custom_call_target="tpu_custom_call" | custom-call | tf_op jit(solution)/shard_map/pallas_call | solution.py:291
  49.7 1.5 %copy.16 = bf16[10,2048]{1,0:T(8,128)(2,1)} copy(bf16[10,2048]{1,0:T(8,128)(2,1)} %shard_map.136) | data formatting | bytes 81920
